TPU v7x, 128 devices: a whole 4x4x4 slice. The times are simulated.
128 devices in a mesh: occ: 4 (over y), vir: 32 (over z, x, core).
Axes of the slice: x: 4, y: 4, z: 4, core: 2. Of those that a mesh axis runs over, the one named last changes fastest.
Arguments:
- amplitudes: float32 [64, 4, 6, 128, 128], P('vir', 'occ'), may hold values from -6 to 6
- tile_cols: int32 [64, 4, 6], P('vir', 'occ'), may hold values from 0 to 7, as said below
- tile_count: int32 [64, 4], P('vir', 'occ'), may hold values from 1 to 6, as said below
- integrals: float32 [4096, 8192], P('occ', 'vir'), may hold values from -0.109375 to 0.109375
- residual_in: float32 [64, 128, 8192], P('vir', 'occ'), may hold values from -6 to 6
Outputs:
- residual_out: float32 [64, 128, 8192], P('vir', 'occ')
Inputs may be any that keep to these rules, and one draw needn't show every extreme that they name: `tile_cols`: the entries of one row tile and one contraction shard are distinct; slots from tile_count onward are unused. `tile_count`: in every draw some row tile has 6 live slots in every contraction shard.
All inputs are finite; a program needn't handle non-finite values.
Results may differ from a plain program's by a relative error of at most 0.0003.
Values sent between devices are 32-bit elements; how exact they have to be, the bound alone decides.
A program may use at most 192 MiB of HBM per device.

v0:
```python
import jax
import jax.numpy as jnp
from jax import lax
from jax.sharding import PartitionSpec as P


def live_tiles(amplitudes, tile_count):
    slot_index = jnp.arange(amplitudes.shape[1], dtype=jnp.int32)
    live = (slot_index[None, :] < tile_count[:, None]).astype(jnp.float32)
    return amplitudes * live[:, :, None, None]


def panel(masked, tile_cols, integral_rows):
    tile = masked.shape[2]
    blocks = integral_rows.reshape(-1, tile, integral_rows.shape[1])
    chosen = blocks[tile_cols]
    return jnp.einsum("rsij,rsjc->ric", masked, chosen, precision=lax.Precision.HIGHEST)


def on_device(amplitudes, tile_cols, tile_count, integrals, residual_in):
    rows_here = amplitudes.shape[0]
    quarter = residual_in.shape[1]
    width = residual_in.shape[2]
    occ_size = lax.axis_size("occ")
    vir_size = lax.axis_size("vir")
    local_cols = tile_cols[:, 0]
    local_count = tile_count[:, 0]
    masked = live_tiles(amplitudes[:, 0], local_count)
    partial_value = panel(masked, local_cols, lax.all_gather(integrals, "vir", axis=1, tiled=True))
    pair_rows = lax.psum_scatter(partial_value, "occ", scatter_dimension=1, tiled=True)
    outgoing = pair_rows.reshape(rows_here, quarter, vir_size, rows_here, occ_size, quarter)
    outgoing = outgoing.transpose(4, 2, 0, 1, 3, 5).reshape(
        occ_size * vir_size, rows_here * quarter * rows_here * quarter
    )
    incoming = lax.all_to_all(outgoing, ("occ", "vir"), split_axis=0, concat_axis=0, tiled=True)
    incoming = incoming.reshape(occ_size, vir_size, rows_here, quarter, rows_here, quarter)
    mirror = incoming.transpose(4, 5, 1, 2, 0, 3).reshape(rows_here, quarter, width)
    return residual_in + pair_rows + mirror


def solution(mesh):
    in_specs = (
        P("vir", "occ", None, None, None),
        P("vir", "occ", None),
        P("vir", "occ"),
        P("occ", "vir"),
        P("vir", "occ", None),
    )
    out_specs = P("vir", "occ", None)
    return jax.shard_map(
        on_device, mesh=mesh, in_specs=in_specs, out_specs=out_specs, check_vma=False
    )
```

profile of v0, /device:TPU:1, one launch (start us, length us, event | category | flops | bytes accessed | tf_op | source)
XLA Modules:
  0.0 432.5 jit_solution(14324324512696304020)
XLA Ops:
  6.5 0.0 all-gather.2.cloned.1.call-start
  6.5 0.7 all-gather.2.cloned.1.call-update
  7.3 0.0 reduce-scatter.2.cloned.1.call-start
  7.3 0.7 compare_select_fusion
  8.0 0.1 reshape.74
  8.1 0.7 compare_convert_fusion
  8.8 130.3 %all-gather.2.cloned.1.call-done = f32[1024,8192]{1,0:T(8,128)} async-done(((f32[1024,256]{1,0:T(8,128)}), f32[1024,8192]{1,0:T(8,128)}) %all-gather.2.cloned.1.call-update) | async-done | bytes 33554448 | tf_op jit(solution)/shard_map/all_gather | solution.py:29
  139.1 21.4 %fusion.9 = (f32[8,128,4096]{2,1,0:T(8,128)}, f32[8,128,4096]{2,1,0:T(8,128)}) fusion(f32[8,128,8192]{2,1,0:T(8,128)} %bitcast.21), kind=kLoop, calls=%fused_computation.15 | loop fusion | bytes 67108864 | tf_op jit(solution)/shard_map/gather | solution.py:16
  160.5 16.3 %gather_fusion = f32[12,128,4096]{2,1,0:T(8,128)} fusion(f32[8,128,4096]{2,1,0:T(8,128)} %get-tuple-element.5, s32[1024]{0:T(1024)S(1)} %pad_clamp_fusion), kind=kCustom, calls=%fused_computation | custom fusion | bytes 50331696 | tf_op jit(solution)/shard_map/gather | solution.py:16
  176.8 0.0 copy-start.1
  176.8 16.3 %gather_fusion.1 = f32[12,128,4096]{2,1,0:T(8,128)} fusion(f32[8,128,4096]{2,1,0:T(8,128)} %get-tuple-element.6, s32[1024]{0:T(1024)S(1)} %pad_clamp_fusion), kind=kCustom, calls=%fused_computation.1 | custom fusion | bytes 50331696 | tf_op jit(solution)/shard_map/gather | solution.py:16
  193.1 0.0 copy-done.1
  193.1 39.6 %fusion.4 = f32[2,128,8192]{2,1,0:T(8,128)} fusion(f32[2,6,128,4096]{3,2,1,0:T(8,128)} %bitcast.18, f32[2,6,128,4096]{3,2,1,0:T(8,128)} %bitcast.17, f32[2,1,6,128,128]{4,3,2,1,0:T(8,128)S(1)} %copy-done.1, f32[2,6]{1,0:T(2,128)S(1)} %compare_convert_fusion), kind=kOutput, calls=%fused_computation.6 | convolution fusion | flops 19340132352 | bytes 59506736 | tf_op jit(solution)/shard_map/rsij,rsjc->ric/dot_general | solution.py:17
  232.6 0.0 reduce-scatter.2.cloned.1.call-update
  232.7 81.3 %reduce-scatter.2.cloned.1.call-done = f32[2,32,8192]{2,1,0:T(8,128)} async-done(((f32[2,128,8192]{2,1,0:T(8,128)}), f32[2,32,8192]{2,1,0:T(8,128)}) %reduce-scatter.2.cloned.1.call-update) | async-done | bytes 2097168 | tf_op jit(solution)/shard_map/reduce_scatter | solution.py:30
  313.9 7.4 %reshape.69 = f32[2,32,32,2,4,32]{5,4,3,2,1,0:T(4,128)} reshape(f32[2,32,8192]{2,1,0:T(8,128)} %reduce-scatter.2.cloned.1.call-done) | data formatting | bytes 4194304 | tf_op jit(solution)/shard_map/reshape | solution.py:31
  321.3 13.2 %copy.13 = f32[2,32,32,2,4,32]{5,3,1,0,2,4:T(2,128)} copy(f32[2,32,32,2,4,32]{5,4,3,2,1,0:T(4,128)} %reshape.69) | data formatting | bytes 4194304 | tf_op jit(solution)/shard_map/reshape | solution.py:31
  334.5 10.1 %all_to_all.8 = f32[128,1,4096]{2,1,0:T(1,128)S(1)} reshape(f32[4,32,2,32,2,32]{5,4,3,2,1,0:T(2,128)} %bitcast.19) | data formatting | bytes 4194304 | tf_op jit(solution)/shard_map/all_to_all | solution.py:35
  344.7 38.4 %all_to_all.10 = f32[128,1,4096]{2,1,0:T(1,128)} all-to-all(f32[128,1,4096]{2,1,0:T(1,128)S(1)} %all_to_all.8), channel_id=1, replica_groups=mesh['occ'=4,'vir'=32] {'occ','vir'}, dimensions={0} | all-to-all | bytes 4194304 | tf_op jit(solution)/shard_map/all_to_all | solution.py:35
  383.1 6.7 %reduce = f32[128,4096]{1,0:T(8,128)S(1)} reduce(f32[128,1,4096]{2,1,0:T(1,128)} %all_to_all.10, f32[]{:T(128)} %constant.8), dimensions={1}, to_apply=%all_to_all.7.reduce_sub_computation | reduce | bytes 4194308 | tf_op jit(solution)/shard_map/all_to_all | solution.py:35
  389.7 8.4 %reshape.70 = f32[4,32,2,32,2,32]{5,4,3,2,1,0:T(2,128)} reshape(f32[128,4096]{1,0:T(8,128)S(1)} %reduce) | data formatting | bytes 4194304 | tf_op jit(solution)/shard_map/reshape | solution.py:36
  398.2 0.0 copy-start
  398.2 13.8 %copy.10 = f32[2,32,32,2,4,32]{5,4,3,2,1,0:T(4,128)} copy(f32[2,32,32,2,4,32]{1,0,5,3,2,4:T(2,128)} %bitcast.20) | data formatting | bytes 4194304 | tf_op jit(solution)/shard_map/transpose | solution.py:37
  412.0 9.9 %reshape.71 = f32[2,32,8192]{2,1,0:T(8,128)} reshape(f32[2,32,32,2,4,32]{5,4,3,2,1,0:T(4,128)} %copy.10) | data formatting | bytes 4194304 | tf_op jit(solution)/shard_map/reshape | solution.py:37
  421.8 0.0 copy-done
  421.8 3.8 add_add_fusion
  (1 shorter events, 0.0 us)
Async XLA Ops:
  6.5 132.6 %all-gather.2.cloned.1.call-start = ((), (), s32[]{:S(2)}) async-start(), calls=%async_computation.2 | async-start | bytes 34603008 | tf_op jit(solution)/shard_map/all_gather | solution.py:29
  7.3 306.7 %reduce-scatter.2.cloned.1.call-start = ((), (), s32[]{:S(2)}) async-start(), calls=%async_computation.3 | async-start | bytes 10485760 | tf_op jit(solution)/shard_map/reduce_scatter | solution.py:30
  176.8 16.3 %copy-start.1 = (f32[2,1,6,128,128]{4,3,2,1,0:T(8,128)S(1)}, f32[2,1,6,128,128]{4,3,2,1,0:T(8,128)}, u32[]{:S(2)}) copy-start(f32[2,1,6,128,128]{4,3,2,1,0:T(8,128)} %param.5) | copy-start | bytes 2359300
  398.2 23.7 %copy-start = (f32[2,32,8192]{2,1,0:T(8,128)S(1)}, f32[2,32,8192]{2,1,0:T(8,128)}, u32[]{:S(2)}) copy-start(f32[2,32,8192]{2,1,0:T(8,128)} %reduce-scatter.2.cloned.1.call-done) | copy-start | bytes 6291460
Sparse Core Ops, SparseCore 0:
  9.5 129.5 all-gather.1
  232.8 81.0 reduce-scatter.1
where the time goes:
time: 433 us
  waiting for transfers between devices  212 us (49%)
  local copies, waits for them, and re-layouts  117 us (27%)
  matrix products  39.6 us (9%)
  blocking collectives  38.4 us (9%)
  between operations  13.4 us (3%)
  other arithmetic  11.9 us (3%)
    all_gather x1, waiting for transfers between devices, on_device(): lax.all_gather(integrals, 'vir', axis=1, tiled=True)  130 us
    reduce_scatter x1, waiting for transfers between devices, on_device(): lax.psum_scatter(partial_value, 'occ', scatter_dimension=1, tiled=True)  81.3 us
    gather x3, local copies, waits for them, and re-layouts, panel(): chosen = blocks[tile_cols]  53.9 us
    dot_general x1, matrix products, panel(): jnp.einsum('rsij,rsjc->ric', masked, chosen, precision=lax.Precision.HIGH...  39.6 us
    all_to_all x1, blocking collectives, on_device(): lax.all_to_all(outgoing, ('occ', 'vir'), split_axis=0, concat_axis=0, til...  38.4 us
    reshape x2, local copies, waits for them, and re-layouts, on_device(): pair_rows.reshape(rows_here, quarter, vir_size, rows_here, occ_size, quar...  20.6 us
    transpose x1, local copies, waits for them, and re-layouts, on_device(): incoming.transpose(4, 5, 1, 2, 0, 3).reshape(rows_here, quarter, width)  13.8 us
    all_to_all x1, local copies, waits for them, and re-layouts, on_device(): lax.all_to_all(outgoing, ('occ', 'vir'), split_axis=0, concat_axis=0, til...  10.1 us
  transfers between devices with their start and end apart: 2, of which 2 were waited for; matrix products, arithmetic and copies ran while one was open for 0% of the time, Pallas kernels for 0%

commit v1 on v0

v1 whole, which is shorter than its diff:
```python
import jax
import jax.numpy as jnp
from jax import lax
from jax.experimental import pallas as pl
from jax.experimental.pallas import tpu as pltpu
from jax.sharding import PartitionSpec as P

MESH = pl.DeviceIdType.MESH
LAG1 = 2
LAG2 = 4
UNITS = 16


def kernel(
    cols_s, count_s, a_ref, b_ref, r_ref, out_ref,
    ab, mb, bb, adh, adl, bh, bl, p, r1, r2, f, ft, direct, stg,
    own_sem, asend, arecv, a2send, msend, mrecv, bsend, brecv, b2send,
    s1send, s1recv, s2send, s2recv, dsend, drecv, tsend, trecv,
):
    y = lax.axis_index("occ")
    v = lax.axis_index("vir")
    z = v // 8
    x = (v // 2) % 4
    k = v % 2
    other = 1 - k
    xm, xp = (x + 3) % 4, (x + 1) % 4
    zm, zp = (z + 3) % 4, (z + 1) % 4

    def vir(zz, xx, kk):
        return zz * 8 + xx * 2 + kk

    sibling = (y, vir(z, x, other))

    def remote(src, dst, send, recv, dev):
        return pltpu.make_async_remote_copy(
            src_ref=src, dst_ref=dst, send_sem=send, recv_sem=recv,
            device_id=dev, device_id_type=MESH,
        )

    barrier = pltpu.get_barrier_semaphore()

    def greet_row(i, c):
        pl.semaphore_signal(barrier, inc=1, device_id=(y, z * 8 + (v % 8 + i) % 8), device_id_type=MESH)
        return c

    def greet_col(i, c):
        n = (y * 4 + z + i) % 16
        pl.semaphore_signal(barrier, inc=1, device_id=(n // 4, vir(n % 4, x, k)), device_id_type=MESH)
        return c

    lax.fori_loop(1, 8, greet_row, 0)
    lax.fori_loop(1, 16, greet_col, 0)

    for t in range(2):
        for s in range(8):
            if s < 6:
                col = jnp.where(s < count_s[t, 0], cols_s[t, 0, s], -1)
                mb[k, t, s, :] = jnp.full((128,), col, jnp.int32)
            else:
                mb[k, t, s, :] = jnp.full((128,), -1, jnp.int32)
    own_a = pltpu.make_async_copy(a_ref, ab.at[0, k], own_sem.at[0])
    own_b = pltpu.make_async_copy(b_ref, bb.at[0], own_sem.at[1])
    own_a.start()
    own_b.start()

    pl.semaphore_wait(barrier, 22)

    sib_a0 = remote(a_ref, ab.at[0, k], asend.at[0], arecv.at[0, k], sibling)
    sib_a0.start()
    left_a = remote(a_ref, ab.at[1, k], asend.at[1], arecv.at[1, k], (y, vir(z, xm, k)))
    right_a = remote(a_ref, ab.at[3, k], asend.at[2], arecv.at[3, k], (y, vir(z, xp, k)))
    left_a.start()
    right_a.start()
    down_b = remote(b_ref, bb.at[1], bsend.at[0], brecv.at[1], (y, vir(zm, x, k)))
    up_b = remote(b_ref, bb.at[3], bsend.at[1], brecv.at[3], (y, vir(zp, x, k)))
    down_b.start()
    up_b.start()

    def send_meta(i, c):
        w = (v % 8 + i) % 8
        remote(
            mb.at[k], mb.at[(x - w // 2 + 4) % 4 * 2 + k], msend, mrecv, (y, z * 8 + w)
        ).start()
        return c

    lax.fori_loop(1, 8, send_meta, 0)

    def wait_for(ref, sem):
        pltpu.make_async_copy(ref, ref, sem).wait()

    own_a.wait()
    own_b.wait()

    def prep_a(d):
        def tile(n, c):
            kk, t = n // 2, n % 2
            rows = pl.ds(pl.multiple_of(t * 128, 128), 128)
            for col in range(8):
                val = jnp.zeros((128, 128), jnp.float32)
                for s in range(6):
                    hit = mb[d * 2 + kk, t, pl.ds(s, 1), :] == col
                    val = jnp.where(hit, ab[d, kk, t, s], val)
                hi = val.astype(jnp.bfloat16)
                lo = (val - hi.astype(jnp.float32)).astype(jnp.bfloat16)
                adh[d, kk, rows, col * 128:(col + 1) * 128] = hi
                adl[d, kk, rows, col * 128:(col + 1) * 128] = lo
            return c

        lax.fori_loop(0, 4, tile, 0)

    def prep_b(d):
        def rows(n, c):
            at = pl.ds(pl.multiple_of(n * 128, 128), 128)
            val = bb[d, at, :]
            hi = val.astype(jnp.bfloat16)
            bh[d, at, :] = hi
            bl[d, at, :] = (val - hi.astype(jnp.float32)).astype(jnp.bfloat16)
            return c

        lax.fori_loop(0, 8, rows, 0)

    def decode(u):
        early = jnp.where(u < 12, 3, u - 12)
        i = jnp.where(u < 9, u % 3, early)
        j = jnp.where(u < 9, u // 3, jnp.where(u < 12, u - 9, 3))
        return i + i // 2 - 2 * (i // 3), j + j // 2 - 2 * (j // 3)

    def pair_bits(q, odd):
        one, two = ((q + 1) // 2) % 2, q // 2
        return one + odd * (two - one), two + odd * (one - two)

    def partners(odd):
        near, far = y + 1 - 2 * (y % 2), 3 - y
        return near + odd * (far - near), far + odd * (near - far)

    def first_stage(u):
        return remote(
            p.at[u, 0], r1.at[u], s1send, s1recv.at[u], (partners(u % 2)[0], v)
        )

    def second_stage(u):
        return remote(
            p.at[u, 1, 0], r2.at[u], s2send, s2recv.at[u], (partners(u % 2)[1], v)
        )

    def compute(u, da, db):
        odd = u % 2
        b1, b2 = pair_bits(y, odd)

        def half(kk, c):
            ah, al = adh[da, kk], adl[da, kk]
            wh, wl = bh[db], bl[db]
            acc = jnp.dot(ah, wh, preferred_element_type=jnp.float32)
            acc += jnp.dot(ah, wl, preferred_element_type=jnp.float32)
            acc += jnp.dot(al, wh, preferred_element_type=jnp.float32)
            for q in range(4):
                q1, q2 = pair_bits(q, odd)
                h = 1 - (q1 + b1) % 2
                w = 1 - (q2 + b2) % 2
                for t in range(2):
                    p[u, h, w, kk * 2 + t] = acc[t * 128 + q * 32:t * 128 + q * 32 + 32]
            return c

        lax.fori_loop(0, 2, half, 0)

    def finish(u):
        da, db = decode(u)
        zz, xx = (z + db) % 4, (x + da) % 4
        total = p[u, 1, 1] + r2[u]
        f[u] = total
        flipped = total.reshape(128, 256).T
        ft[u] = flipped.reshape(2, 4, 32, 128)
        columns = pl.ds(pl.multiple_of(vir(zz, x, k) * 256, 256), 256)
        for kk in range(2):
            src = f.at[u, pl.ds(kk * 2, 2)]
            dst = direct.at[:, :, columns]
            here = jnp.logical_and(da == 0, k == kk)

            @pl.when(here)
            def _():
                pltpu.make_async_copy(src, dst, drecv).start()

            @pl.when(jnp.logical_not(here))
            def _():
                remote(src, dst, dsend, drecv, (y, vir(z, xx, kk))).start()

        place = y * 16 + z * 4 + xx
        for q in range(4):
            src = ft.at[u, :, q]
            dst = stg.at[place]
            here = jnp.logical_and(db == 0, y == q)

            @pl.when(here)
            def _():
                pltpu.make_async_copy(src, dst, trecv).start()

            @pl.when(jnp.logical_not(here))
            def _():
                remote(src, dst, tsend, trecv, (q, vir(zz, x, k))).start()

    fwd_a1 = remote(ab.at[1, k], ab.at[1, k], asend.at[3], arecv.at[1, k], sibling)
    fwd_a3 = remote(ab.at[3, k], ab.at[3, k], asend.at[4], arecv.at[3, k], sibling)
    fwd_a2 = remote(ab.at[2, k], ab.at[2, k], asend.at[5], arecv.at[2, k], sibling)
    far_a1 = remote(ab.at[1, k, 0], ab.at[2, k, 0], a2send.at[0], arecv.at[2, k], (y, vir(z, xm, k)))
    far_a3 = remote(ab.at[3, k, 1], ab.at[2, k, 1], a2send.at[1], arecv.at[2, k], (y, vir(z, xp, k)))
    low, high = pl.ds(0, 512), pl.ds(512, 512)
    far_b1 = remote(bb.at[1, low], bb.at[2, low], b2send.at[0], brecv.at[2], (y, vir(zm, x, k)))
    far_b3 = remote(bb.at[3, high], bb.at[2, high], b2send.at[1], brecv.at[2], (y, vir(zp, x, k)))

    def step(s, c):
        @pl.when(s < UNITS)
        def _():
            da, db = decode(s)

            @pl.when(s == 0)
            def _():
                wait_for(mb.at[pl.ds(0, 7)], mrecv)
                wait_for(ab.at[0, other], arecv.at[0, other])

            @pl.when(s == 1)
            def _():
                wait_for(ab.at[1, k], arecv.at[1, k])
                far_a1.start()
                fwd_a1.start()
                wait_for(ab.at[3, k], arecv.at[3, k])
                far_a3.start()
                fwd_a3.start()
                wait_for(ab.at[1, other], arecv.at[1, other])

            @pl.when(s == 2)
            def _():
                wait_for(ab.at[3, other], arecv.at[3, other])

            @pl.when(s == 3)
            def _():
                wait_for(bb.at[1], brecv.at[1])
                far_b1.start()
                wait_for(bb.at[3], brecv.at[3])
                far_b3.start()

            @pl.when(s == 8)
            def _():
                wait_for(ab.at[2, k], arecv.at[2, k])
                fwd_a2.start()

            @pl.when(s == 9)
            def _():
                wait_for(ab.at[2, other], arecv.at[2, other])

            @pl.when(s == 12)
            def _():
                wait_for(bb.at[2], brecv.at[2])

            @pl.when(jnp.logical_or(s < 3, s == 9))
            def _():
                prep_a(da)

            @pl.when(jnp.logical_or(jnp.logical_and(s < 7, s % 3 == 0), s == 12))
            def _():
                prep_b(db)

            compute(s, da, db)
            first_stage(s).start()

        @pl.when(jnp.logical_and(s >= LAG1, s < LAG1 + UNITS))
        def _():
            u = s - LAG1
            first_stage(u).wait_recv()
            p[u, 1] += r1[u]
            second_stage(u).start()

        @pl.when(s >= LAG2)
        def _():
            u = s - LAG2
            second_stage(u).wait_recv()
            finish(u)

        return c

    lax.fori_loop(0, UNITS + LAG2, step, 0)

    for copy in (sib_a0, left_a, right_a, fwd_a1, fwd_a3, fwd_a2, far_a1, far_a3, down_b, up_b, far_b1, far_b3):
        copy.wait_send()
    wait_for(mb.at[pl.ds(0, 7)], msend)
    wait_for(r1, s1send)
    wait_for(r2, s2send)
    wait_for(direct.at[:, :, pl.ds(0, 7168)], dsend)
    wait_for(stg.at[pl.ds(0, 60)], tsend)

    wait_for(direct, drecv)
    wait_for(stg, trecv)
    group = lax.broadcasted_iota(jnp.int32, (32, 128), 1) // 32

    def assemble(g, c):
        for t in range(2):
            parts = [stg[16 * n + g, t] for n in range(4)]
            for n in range(4):
                merged = parts[n]
                for src in range(4):
                    if src != n:
                        merged = jnp.where(group == src, pltpu.roll(parts[src], (32 * (src - n)) % 128, 1), merged)
                columns = pl.ds(pl.multiple_of(g * 512 + n * 128, 128), 128)
                out_ref[t, :, columns] = r_ref[t, :, columns] + direct[t, :, columns] + merged
        return c

    lax.fori_loop(0, 16, assemble, 0)


def on_device(amplitudes, tile_cols, tile_count, integrals, residual_in):
    vmem = pl.BlockSpec(memory_space=pltpu.VMEM)
    smem = pl.BlockSpec(memory_space=pltpu.SMEM)
    f32, bf16 = jnp.float32, jnp.bfloat16
    dma = pltpu.SemaphoreType.DMA
    return pl.pallas_call(
        kernel,
        out_shape=jax.ShapeDtypeStruct(residual_in.shape, f32),
        in_specs=[smem, smem, vmem, vmem, vmem],
        out_specs=vmem,
        scratch_shapes=[
            pltpu.VMEM((4, 2, 2, 6, 128, 128), f32),
            pltpu.VMEM((8, 2, 8, 128), jnp.int32),
            pltpu.VMEM((4, 1024, 256), f32),
            pltpu.VMEM((4, 2, 256, 1024), bf16),
            pltpu.VMEM((4, 2, 256, 1024), bf16),
            pltpu.VMEM((4, 1024, 256), bf16),
            pltpu.VMEM((4, 1024, 256), bf16),
            pltpu.VMEM((UNITS, 2, 2, 4, 32, 256), f32),
            pltpu.VMEM((UNITS, 2, 4, 32, 256), f32),
            pltpu.VMEM((UNITS, 4, 32, 256), f32),
            pltpu.VMEM((UNITS, 4, 32, 256), f32),
            pltpu.VMEM((UNITS, 2, 4, 32, 128), f32),
            pltpu.VMEM((2, 32, 8192), f32),
            pltpu.VMEM((64, 2, 32, 128), f32),
            dma((2,)), dma((6,)), dma((4, 2)), dma((2,)), dma, dma, dma((2,)), dma((4,)), dma((2,)),
            dma, dma((UNITS,)), dma, dma((UNITS,)), dma, dma, dma, dma,
        ],
        compiler_params=pltpu.CompilerParams(
            collective_id=0, has_side_effects=True, vmem_limit_bytes=60 * 1024 * 1024
        ),
        cost_estimate=pl.CostEstimate(flops=10 * 10**9, bytes_accessed=6 * 10**6, transcendentals=0),
    )(tile_cols, tile_count, amplitudes[:, 0], integrals, residual_in)


def solution(mesh):
    in_specs = (
        P("vir", "occ", None, None, None),
        P("vir", "occ", None),
        P("vir", "occ"),
        P("occ", "vir"),
        P("vir", "occ", None),
    )
    out_specs = P("vir", "occ", None)
    return jax.shard_map(
        on_device, mesh=mesh, in_specs=in_specs, out_specs=out_specs, check_vma=False
    )
```

time: 433 us -> 143 us (0.33)
  waiting for transfers between devices: 212 us -> 0 us
  Pallas kernels: 0 us -> 138 us
  local copies, waits for them, and re-layouts: 117 us -> 4.36 us
  matrix products: 39.6 us -> 0 us
  blocking collectives: 38.4 us -> 0 us
  between operations: 13.4 us -> 0.01 us
  other arithmetic: 11.9 us -> 0 us
    pallas_call x0 -> x1, Pallas kernels: none -> 138 us  [on_device(): pl.pallas_call(kernel, out_shape=jax.ShapeDtypeStruct(residual_in.shape,...]
    all_gather x1 -> x0, waiting for transfers between devices: 130 us -> none  [on_device(): lax.all_gather(integrals, 'vir', axis=1, tiled=True)]
    reduce_scatter x1 -> x0, waiting for transfers between devices: 81.3 us -> none  [on_device(): lax.psum_scatter(partial_value, 'occ', scatter_dimension=1, tiled=True)]
    gather x3 -> x0, local copies, waits for them, and re-layouts: 53.9 us -> none  [panel(): chosen = blocks[tile_cols]]
    dot_general x1 -> x0, matrix products: 39.6 us -> none  [panel(): jnp.einsum('rsij,rsjc->ric', masked, chosen, precision=lax.Precision.HIGH...]
    reshape x4 -> x0, local copies, waits for them, and re-layouts: 38.9 us -> none  [the longest x2 20.6 us: on_device(): pair_rows.reshape(rows_here, quarter, vir_size, rows_here, occ_size, quar...]
    all_to_all x1 -> x0, blocking collectives: 38.4 us -> none  [on_device(): lax.all_to_all(outgoing, ('occ', 'vir'), split_axis=0, concat_axis=0, til...]
    transpose x1 -> x0, local copies, waits for them, and re-layouts: 13.8 us -> none  [on_device(): incoming.transpose(4, 5, 1, 2, 0, 3).reshape(rows_here, quarter, width)]
  transfers between devices with their start and end apart: 2 -> 0, of which waited for: 2 -> 0; matrix products, arithmetic and copies ran while one was open for 0% -> 0% of each run, Pallas kernels for 0% -> 0%
where the time goes in v1:
time: 143 us
  Pallas kernels  138 us (97%)
  local copies, waits for them, and re-layouts  4.36 us (3%)
    pallas_call x1, Pallas kernels, on_device(): pl.pallas_call(kernel, out_shape=jax.ShapeDtypeStruct(residual_in.shape,...  138 us
    unnamed x2, local copies, waits for them, and re-layouts  4.36 us

profile of v1, /device:TPU:1, one launch (start us, length us, event | category | flops | bytes accessed | tf_op | source)
XLA Modules:
  0.0 142.8 jit_solution(2555691596088971118)
XLA Ops:
  0.0 1.3 copy.6.count_s
  1.3 138.4 %shard_map.55 = f32[2,32,8192]{2,1,0:T(8,128)} custom-call(s32[2,1,6]{2,1,0:T(1,128)} %cols_s.1, s32[2,1]{1,0:T(2,128)} %copy.6.count_s, f32[2,6,128,128]{3,2,1,0:T(8,128)} %bitcast.1, f32[1024,256]{1,0:T(8,128)} %b_ref.1, f32[2,32,8192]{2,1,0:T(8,128)} %r_ref.1), custom_call_target="tpu_custom_call" | custom-call | flops 10000000000 | bytes 6000000 | tf_op jit(solution)/shard_map/pallas_call | solution.py:314
  139.7 3.1 %copy.8 = f32[2,32,8192]{2,1,0:T(8,128)} copy(f32[2,32,8192]{2,1,0:T(8,128)} %shard_map.55) | data formatting | bytes 4194304

commit v2 on v1

v2 whole, which is shorter than its diff:
```python
import jax
import jax.numpy as jnp
from jax import lax
from jax.experimental import pallas as pl
from jax.experimental.pallas import tpu as pltpu
from jax.sharding import PartitionSpec as P

MESH = pl.DeviceIdType.MESH
LAG1 = 2
LAG2 = 4
DX = (0, 1, 3, 2, 0, 2, 0, 1, 1, 1, 2)
DZ = (0, 0, 0, 0, 2, 2, 1, 1, 3, 2, 1)
BOTH = (1, 0, 0, 0, 0, 0, 1, 1, 1, 1, 1)
TURN = (0, 1, 1, 1, 1, 1, 1, 1, 1, 1, 1)
A_FROM = (0, 2, 6, 4, 0, 0, 8, 0, 10, 9, 0)
A_TO = (2, 4, 8, 6, 0, 0, 9, 0, 11, 10, 0)
B_FROM = (0, 0, 0, 0, 7, 0, 6, 2, 8, 0, 4)
B_TO = (2, 0, 0, 0, 8, 0, 7, 4, 9, 0, 6)
UNITS = len(DX)


def table(n, values):
    out = jnp.int32(values[0])
    for i in range(1, len(values)):
        if values[i] != values[0]:
            out = jnp.where(n == i, values[i], out)
    return out


def covers():
    direct = {(-a % 4, b) for a, b in zip(DX, DZ)}
    turned = {(a, -b % 4) for a, b, t in zip(DX, DZ, TURN) if t}
    return direct & turned, direct - turned, turned - direct


def kernel(
    cols_s, count_s, a_ref, b_ref, out_ref,
    ab, mb, bb, relay, adh, adl, bh, bl, p, r1, r2, ft, direct, stg,
    own_sem, asend, arecv, a2send, a2recv, msend, mrecv, bsend, brecv, b2send, b2recv, rsend, rrecv,
    s1send, s1recv, s2send, s2recv, dsend, drecv, tsend, trecv,
):
    y = lax.axis_index("occ")
    v = lax.axis_index("vir")
    z = v // 8
    x = (v // 2) % 4
    k = v % 2
    other = 1 - k
    xm, xp = (x + 3) % 4, (x + 1) % 4
    zm, zp = (z + 3) % 4, (z + 1) % 4

    def vir(zz, xx, kk):
        return zz * 8 + xx * 2 + kk

    sibling = (y, vir(z, x, other))

    def remote(src, dst, send, recv, dev):
        return pltpu.make_async_remote_copy(
            src_ref=src, dst_ref=dst, send_sem=send, recv_sem=recv,
            device_id=dev, device_id_type=MESH,
        )

    barrier = pltpu.get_barrier_semaphore()

    def greet_row(i, c):
        pl.semaphore_signal(barrier, inc=1, device_id=(y, z * 8 + (v % 8 + i) % 8), device_id_type=MESH)
        return c

    def greet_col(i, c):
        n = (y * 4 + z + i) % 16
        pl.semaphore_signal(barrier, inc=1, device_id=(n // 4, vir(n % 4, x, k)), device_id_type=MESH)
        return c

    lax.fori_loop(1, 8, greet_row, 0)
    lax.fori_loop(1, 16, greet_col, 0)

    for t in range(2):
        for s in range(8):
            if s < 6:
                col = jnp.where(s < count_s[t, 0], cols_s[t, 0, s], -1)
                mb[k, t, s, :] = jnp.full((128,), col, jnp.int32)
            else:
                mb[k, t, s, :] = jnp.full((128,), -1, jnp.int32)
    own_a = pltpu.make_async_copy(a_ref, ab.at[k], own_sem.at[0])
    own_b = pltpu.make_async_copy(b_ref, bb.at[k], own_sem.at[1])
    own_a.start()
    own_b.start()

    def wait_for(ref, sem):
        pltpu.make_async_copy(ref, ref, sem).wait()

    pl.semaphore_wait(barrier, 22)

    def meta_row(i, c):
        w = (v % 8 + i) % 8
        remote(
            mb.at[k], mb.at[(x - w // 2 + 4) % 4 * 2 + k], msend, mrecv, (y, z * 8 + w)
        ).start()
        return c

    def meta_col(i, c):
        remote(mb.at[k], mb.at[11 - i], msend, mrecv, (y, vir((z + i) % 4, x, k))).start()
        return c

    lax.fori_loop(1, 8, meta_row, 0)
    lax.fori_loop(1, 4, meta_col, 0)

    left, right = (y, vir(z, xm, k)), (y, vir(z, xp, k))
    below, above = (y, vir(zm, x, k)), (y, vir(zp, x, k))
    low, high = pl.ds(0, 512), pl.ds(512, 512)
    one, two, three = 2 + k, 4 + k, 6 + k

    def ahop(n, src, slot, dev):
        return remote(src, ab.at[slot], asend.at[n], arecv.at[slot], dev)

    def bhop(n, src, slot, dev):
        return remote(src, bb.at[slot], bsend.at[n], brecv.at[slot], dev)

    def ahalf(n, src, slot, t, dev):
        return remote(ab.at[src, t], ab.at[slot, t], a2send.at[n], a2recv.at[n], dev)

    def bhalf(n, src, slot, part, dev):
        return remote(src, bb.at[slot, part], b2send.at[n], b2recv.at[n], dev)

    sib_a0 = ahop(0, a_ref, k, sibling)
    sib_b0 = bhop(0, b_ref, k, sibling)
    a_left = ahop(1, a_ref, one, left)
    a_right = ahop(2, a_ref, three, right)
    a_below = ahop(3, a_ref, 8, below)
    a_above = ahop(4, a_ref, 10, above)
    sib_a1 = ahop(5, ab.at[one], one, sibling)
    sib_a3 = ahop(6, ab.at[three], three, sibling)
    sib_a2 = ahop(7, ab.at[two], two, sibling)
    b_left = bhop(1, b_ref, one, left)
    b_below = bhop(2, b_ref, 6, below)
    b_above = bhop(3, b_ref, 8, above)
    sib_b1 = bhop(4, bb.at[one], one, sibling)
    sib_b2 = bhop(5, bb.at[two], two, sibling)
    far_a1 = ahalf(0, one, two, 0, left)
    far_a3 = ahalf(1, three, two, 1, right)
    far_az1 = ahalf(2, 8, 9, 0, below)
    far_az3 = ahalf(3, 10, 9, 1, above)
    far_bz1 = bhalf(0, bb.at[6, low], 7, low, below)
    far_bz3 = bhalf(1, bb.at[8, high], 7, high, above)
    far_b1 = bhalf(2, bb.at[one, low], two, low, left)
    far_b3 = bhalf(3, relay, two, high, right)
    b_relay = remote(b_ref.at[high], relay, rsend, rrecv, right)
    sends = (
        sib_a0, sib_b0, a_left, a_right, a_below, a_above, sib_a1, sib_a3, sib_a2,
        b_left, b_below, b_above, sib_b1, sib_b2, far_a1, far_a3, far_az1, far_az3,
        far_bz1, far_bz3, far_b1, far_b3, b_relay,
    )

    def got_a(slot):
        wait_for(ab.at[slot], arecv.at[slot])

    def got_b(slot):
        wait_for(bb.at[slot], brecv.at[slot])

    sib_a0.start()
    sib_b0.start()
    a_left.start()
    a_right.start()
    b_below.start()
    b_above.start()
    own_a.wait()
    own_b.wait()

    def prep_a(d, c):
        def tile(t, c):
            rows = pl.ds(pl.multiple_of(t * 128, 128), 128)
            for col in range(8):
                val = jnp.zeros((128, 128), jnp.float32)
                for s in range(6):
                    hit = mb[d, t, pl.ds(s, 1), :] == col
                    val = jnp.where(hit, ab[d, t, s], val)
                hi = val.astype(jnp.bfloat16)
                lo = (val - hi.astype(jnp.float32)).astype(jnp.bfloat16)
                adh[d, rows, col * 128:(col + 1) * 128] = hi
                adl[d, rows, col * 128:(col + 1) * 128] = lo
            return c

        return lax.fori_loop(0, 2, tile, c)

    def prep_b(d, c):
        def rows(n, c):
            at = pl.ds(pl.multiple_of(n * 128, 128), 128)
            val = bb[d, at, :]
            hi = val.astype(jnp.bfloat16)
            bh[d, at, :] = hi
            bl[d, at, :] = (val - hi.astype(jnp.float32)).astype(jnp.bfloat16)
            return c

        return lax.fori_loop(0, 8, rows, c)

    def pair_bits(q, odd):
        one, two = ((q + 1) // 2) % 2, q // 2
        return one + odd * (two - one), two + odd * (one - two)

    def partners(odd):
        near, far = y + 1 - 2 * (y % 2), 3 - y
        return near + odd * (far - near), far + odd * (near - far)

    def first_stage(u):
        return remote(
            p.at[u, 0], r1.at[u], s1send, s1recv.at[u], (partners(u % 2)[0], v)
        )

    def second_stage(u):
        return remote(
            p.at[u, 1, 0], r2.at[u], s2send, s2recv.at[u], (partners(u % 2)[1], v)
        )

    def product(sa, sb):
        ah, al, wh, wl = adh[sa], adl[sa], bh[sb], bl[sb]
        acc = jnp.dot(ah, wh, preferred_element_type=jnp.float32)
        acc += jnp.dot(ah, wl, preferred_element_type=jnp.float32)
        return acc + jnp.dot(al, wh, preferred_element_type=jnp.float32)

    def compute(u):
        da, db = table(u, DX), table(u, DZ)
        odd = u % 2
        b1, b2 = pair_bits(y, odd)
        column_a = jnp.where(db == 0, k, 7 + db)
        column_b = jnp.where(db == 0, k, 5 + db)

        def places():
            for q in range(4):
                q1, q2 = pair_bits(q, odd)
                for t in range(2):
                    yield 1 - (q1 + b1) % 2, 1 - (q2 + b2) % 2, t, t * 128 + q * 32

        def half(kk, c):
            acc = product(da * 2 + kk, column_b)
            for h, w, t, row in places():
                p[u, h, w, kk * 2 + t] = acc[row:row + 32]
            return c

        def turned(kk, c):
            acc = product(column_a, da * 2 + kk).T
            for h, w, t, row in places():
                p[u, h, w, kk * 2 + t] += acc[row:row + 32]
            return c

        lax.fori_loop(0, 2, half, 0)
        lax.fori_loop(0, 2 * table(u, BOTH), turned, 0)

    def finish(u):
        da, db = table(u, DX), table(u, DZ)
        zz, xx = (z + db) % 4, (x + da) % 4
        total = p[u, 1, 1] + r2[u]
        p[u, 1, 1] = total
        columns = pl.ds(pl.multiple_of(vir(zz, x, k) * 256, 256), 256)
        for kk in range(2):
            src = p.at[u, 1, 1, pl.ds(kk * 2, 2)]
            dst = direct.at[:, :, columns]
            here = jnp.logical_and(da == 0, k == kk)

            @pl.when(here)
            def _():
                pltpu.make_async_copy(src, dst, drecv).start()

            @pl.when(jnp.logical_not(here))
            def _():
                remote(src, dst, dsend, drecv, (y, vir(z, xx, kk))).start()

        place = y * 16 + z * 4 + xx

        @pl.when(table(u, TURN) == 1)
        def _():
            ft[u] = total.reshape(128, 256).T.reshape(2, 4, 32, 128)
            for q in range(4):
                src = ft.at[u, :, q]
                dst = stg.at[place]
                here = jnp.logical_and(db == 0, y == q)

                @pl.when(here)
                def _():
                    pltpu.make_async_copy(src, dst, trecv).start()

                @pl.when(jnp.logical_not(here))
                def _():
                    remote(src, dst, tsend, trecv, (q, vir(zz, x, k))).start()

    def step(s, c):
        @pl.when(s < UNITS)
        def _():
            @pl.when(s == 0)
            def _():
                wait_for(mb.at[pl.ds(0, 10)], mrecv)
                got_a(other)
                got_b(other)

            @pl.when(s == 1)
            def _():
                got_a(one)
                far_a1.start()
                sib_a1.start()
                got_a(three)
                far_a3.start()
                sib_a3.start()
                got_a(2 + other)

            @pl.when(s == 2)
            def _():
                got_a(6 + other)
                got_b(6)
                far_bz1.start()
                got_b(8)
                far_bz3.start()

            @pl.when(s == 3)
            def _():
                far_a1.wait_recv()
                far_a3.wait_recv()
                sib_a2.start()
                b_left.start()
                b_relay.start()
                got_a(4 + other)

            @pl.when(s == 4)
            def _():
                far_bz1.wait_recv()
                far_bz3.wait_recv()
                a_below.start()
                a_above.start()

            @pl.when(s == 6)
            def _():
                b_relay.wait_recv()
                far_b3.start()
                got_b(one)
                far_b1.start()
                sib_b1.start()
                got_a(8)
                far_az1.start()
                got_a(10)
                far_az3.start()

            @pl.when(s == 7)
            def _():
                got_b(2 + other)

            @pl.when(s == 9)
            def _():
                far_az1.wait_recv()
                far_az3.wait_recv()
                far_b1.wait_recv()
                far_b3.wait_recv()
                sib_b2.start()

            @pl.when(s == 10)
            def _():
                got_b(4 + other)

            lax.fori_loop(table(s, A_FROM), table(s, A_TO), prep_a, 0)
            lax.fori_loop(table(s, B_FROM), table(s, B_TO), prep_b, 0)
            compute(s)
            first_stage(s).start()

        @pl.when(jnp.logical_and(s >= LAG1, s < LAG1 + UNITS))
        def _():
            u = s - LAG1
            first_stage(u).wait_recv()
            p[u, 1] += r1[u]
            second_stage(u).start()

        @pl.when(s >= LAG2)
        def _():
            u = s - LAG2
            second_stage(u).wait_recv()
            finish(u)

        return c

    lax.fori_loop(0, UNITS + LAG2, step, 0)

    for copy in sends:
        copy.wait_send()
    wait_for(mb.at[pl.ds(0, 10)], msend)
    wait_for(r1, s1send)
    wait_for(r2, s2send)
    home = sum(1 for a in DX if a == 0)
    turned_home = sum(1 for b, t in zip(DZ, TURN) if b == 0 and t)
    wait_for(direct.at[:, :, pl.ds(0, (2 * UNITS - home) * 256)], dsend)
    wait_for(stg.at[pl.ds(0, 4 * sum(TURN) - turned_home)], tsend)

    wait_for(direct.at[:, :, pl.ds(0, UNITS * 512)], drecv)
    wait_for(stg.at[pl.ds(0, 4 * sum(TURN))], trecv)
    group = lax.broadcasted_iota(jnp.int32, (32, 128), 1) // 32
    summed, _, only_turned = covers()

    def assemble(pairs, add):
        pairs = sorted(pairs)

        def body(n, c):
            xx = (x + table(n, [a for a, _ in pairs])) % 4
            zz = (z + table(n, [b for _, b in pairs])) % 4
            g = zz * 4 + xx
            for t in range(2):
                parts = [stg[16 * n + g, t] for n in range(4)]
                for n in range(4):
                    merged = parts[n]
                    for src in range(4):
                        if src != n:
                            merged = jnp.where(group == src, pltpu.roll(parts[src], (32 * (src - n)) % 128, 1), merged)
                    columns = pl.ds(pl.multiple_of(g * 512 + n * 128, 128), 128)
                    direct[t, :, columns] = direct[t, :, columns] + merged if add else merged
            return c

        if pairs:
            lax.fori_loop(0, len(pairs), body, 0)

    assemble(summed, True)
    assemble(only_turned, False)
    out = pltpu.make_async_copy(direct, out_ref, own_sem.at[0])
    out.start()
    out.wait()


def on_device(amplitudes, tile_cols, tile_count, integrals, residual_in):
    vmem = pl.BlockSpec(memory_space=pltpu.VMEM)
    smem = pl.BlockSpec(memory_space=pltpu.SMEM)
    f32, bf16 = jnp.float32, jnp.bfloat16
    dma = pltpu.SemaphoreType.DMA
    added = pl.pallas_call(
        kernel,
        out_shape=jax.ShapeDtypeStruct(residual_in.shape, f32),
        in_specs=[smem, smem, vmem, vmem],
        out_specs=pl.BlockSpec(memory_space=pl.ANY),
        scratch_shapes=[
            pltpu.VMEM((11, 2, 6, 128, 128), f32),
            pltpu.VMEM((11, 2, 8, 128), jnp.int32),
            pltpu.VMEM((9, 1024, 256), f32),
            pltpu.VMEM((512, 256), f32),
            pltpu.VMEM((11, 256, 1024), bf16),
            pltpu.VMEM((11, 256, 1024), bf16),
            pltpu.VMEM((9, 1024, 256), bf16),
            pltpu.VMEM((9, 1024, 256), bf16),
            pltpu.VMEM((UNITS, 2, 2, 4, 32, 256), f32),
            pltpu.VMEM((UNITS, 2, 4, 32, 256), f32),
            pltpu.VMEM((UNITS, 4, 32, 256), f32),
            pltpu.VMEM((UNITS, 2, 4, 32, 128), f32),
            pltpu.VMEM((2, 32, 8192), f32),
            pltpu.VMEM((64, 2, 32, 128), f32),
            dma((2,)), dma((8,)), dma((11,)), dma((4,)), dma((4,)), dma, dma,
            dma((6,)), dma((9,)), dma((4,)), dma((4,)), dma, dma,
            dma, dma((UNITS,)), dma, dma((UNITS,)), dma, dma, dma, dma,
        ],
        compiler_params=pltpu.CompilerParams(
            collective_id=0, has_side_effects=True, vmem_limit_bytes=60 * 1024 * 1024
        ),
        cost_estimate=pl.CostEstimate(flops=10 * 10**9, bytes_accessed=6 * 10**6, transcendentals=0),
    )(tile_cols, tile_count, amplitudes[:, 0], integrals)
    return residual_in + added


def solution(mesh):
    in_specs = (
        P("vir", "occ", None, None, None),
        P("vir", "occ", None),
        P("vir", "occ"),
        P("occ", "vir"),
        P("vir", "occ", None),
    )
    out_specs = P("vir", "occ", None)
    return jax.shard_map(
        on_device, mesh=mesh, in_specs=in_specs, out_specs=out_specs, check_vma=False
    )
```

time: 143 us -> 119 us (0.83)
  Pallas kernels: 138 us -> 114 us
  other arithmetic: 0 us -> 3.12 us
  local copies, waits for them, and re-layouts: 4.36 us -> 1.3 us
    pallas_call x1, Pallas kernels: 138 us -> 114 us  [on_device(): pl.pallas_call(kernel, out_shape=jax.ShapeDtypeStruct(residual_in.shape,...]
    add x0 -> x1, other arithmetic: none -> 3.12 us  [on_device(): return residual_in + added]
    unnamed x2 -> x3, local copies, waits for them, and re-layouts: 4.36 us -> 1.3 us
where the time goes in v2:
time: 119 us; the launch traced here: 118 us
  Pallas kernels  114 us (96%)
  other arithmetic  3.12 us (3%)
  local copies, waits for them, and re-layouts  1.3 us (1%)
    pallas_call x1, Pallas kernels, on_device(): pl.pallas_call(kernel, out_shape=jax.ShapeDtypeStruct(residual_in.shape,...  114 us
    add x1, other arithmetic, on_device(): return residual_in + added  3.12 us

profile of v2, /device:TPU:1, one launch (start us, length us, event | category | flops | bytes accessed | tf_op | source)
XLA Modules:
  0.0 118.4 jit_solution(18327492345178591930)
XLA Ops:
  0.0 1.3 %copy.6.count_s = s32[2,1]{1,0:T(2,128)} copy(s32[2,1]{0,1:T(1,128)} %param.7) | data formatting | bytes 16 | tf_op args[2]
  1.3 0.0 copy-start
  1.3 113.9 %shard_map.55 = f32[2,32,8192]{2,1,0:T(8,128)} custom-call(s32[2,1,6]{2,1,0:T(1,128)} %cols_s.1, s32[2,1]{1,0:T(2,128)} %copy.6.count_s, f32[2,6,128,128]{3,2,1,0:T(8,128)} %bitcast.1, f32[1024,256]{1,0:T(8,128)} %b_ref.1), custom_call_target="tpu_custom_call" | custom-call | flops 10000000000 | bytes 6000000 | tf_op jit(solution)/shard_map/pallas_call | solution.py:425
  115.3 0.0 copy-done
  115.3 3.1 %add.3 = f32[2,32,8192]{2,1,0:T(8,128)} add(f32[2,32,8192]{2,1,0:T(8,128)S(1)} %copy-done, f32[2,32,8192]{2,1,0:T(8,128)} %shard_map.55) | non-fusion elementwise | flops 524288 | bytes 6291456 | tf_op jit(solution)/shard_map/add | solution.py:454
Async XLA Ops:
  1.3 114.0 %copy-start = (f32[2,32,8192]{2,1,0:T(8,128)S(1)}, f32[2,32,8192]{2,1,0:T(8,128)}, u32[]{:S(2)}) copy-start(f32[2,32,8192]{2,1,0:T(8,128)} %param.9) | copy-start | bytes 6291460

commit v3 on v2

v3 whole, which is shorter than its diff:
```python
import jax
import jax.numpy as jnp
from jax import lax
from jax.experimental import pallas as pl
from jax.experimental.pallas import tpu as pltpu
from jax.sharding import PartitionSpec as P

MESH = pl.DeviceIdType.MESH
LAG1 = 2
LAG2 = 4
DX = (0, 0, 1, 3, 1, 3, 2, 2, 0, 0, 2, 2, 0, 0, 1, 1, 1, 1, 1, 1, 2, 2)
DZ = (0, 0, 0, 0, 0, 0, 0, 0, 2, 2, 2, 2, 1, 1, 1, 1, 3, 3, 2, 2, 1, 1)
DT = (0, 1, 0, 0, 1, 1, 0, 1, 0, 1, 0, 1, 0, 1, 0, 1, 0, 1, 0, 1, 0, 1)
MATE = tuple(
    next(j for j in range(len(DX)) if j != i and DX[j] == DX[i] and DZ[j] == DZ[i])
    for i in range(len(DX))
)
BOTH = (1, 1) + (0,) * 10 + (1,) * 10
TURN = (0, 0) + DT[2:]
A_ROWS = {0: 0, 1: 1, 2: 2, 3: 6, 4: 3, 5: 7, 6: 4, 7: 5}
A_SIDE = {0: 0, 12: 1, 16: 3, 18: 2}
B_ROWS = {0: 0, 14: 1, 20: 2}
B_SIDE = {0: 0, 8: 2, 12: 1, 16: 3}
UNITS = len(DX)


def table(n, values):
    out = jnp.int32(values[0])
    for i in range(1, len(values)):
        if values[i] != values[0]:
            out = jnp.where(n == i, values[i], out)
    return out


def planned(n, plan):
    return table(n, [plan.get(i, -1) for i in range(UNITS)])


def covers():
    direct = {(-a % 4, b) for a, b in zip(DX, DZ)}
    turned = {(a, -b % 4) for a, b, t in zip(DX, DZ, TURN) if t}
    return direct & turned, direct - turned, turned - direct


def kernel(
    cols_s, count_s, a_ref, b_ref, out_ref,
    ab, mb, bb, relay, aph, apl, aqh, aql, bph, bpl, bqh, bql, p, r1, r2, ft, direct, stg,
    own_sem, asend, arecv, a2send, a2recv, msend, mrecv, nsend, nrecv, bsend, brecv, b2send, b2recv, rsend, rrecv,
    s1send, s1recv, s2send, s2recv, dsend, drecv, tsend, trecv,
):
    y = lax.axis_index("occ")
    v = lax.axis_index("vir")
    z = v // 8
    x = (v // 2) % 4
    k = v % 2
    other = 1 - k
    xm, xp = (x + 3) % 4, (x + 1) % 4
    zm, zp = (z + 3) % 4, (z + 1) % 4

    def vir(zz, xx, kk):
        return zz * 8 + xx * 2 + kk

    sibling = (y, vir(z, x, other))

    def remote(src, dst, send, recv, dev):
        return pltpu.make_async_remote_copy(
            src_ref=src, dst_ref=dst, send_sem=send, recv_sem=recv,
            device_id=dev, device_id_type=MESH,
        )

    barrier = pltpu.get_barrier_semaphore()

    def greet_row(i, c):
        pl.semaphore_signal(barrier, inc=1, device_id=(y, z * 8 + (v % 8 + i) % 8), device_id_type=MESH)
        return c

    def greet_col(i, c):
        n = (y * 4 + z + i) % 16
        pl.semaphore_signal(barrier, inc=1, device_id=(n // 4, vir(n % 4, x, k)), device_id_type=MESH)
        return c

    lax.fori_loop(1, 8, greet_row, 0)
    lax.fori_loop(1, 16, greet_col, 0)

    for t in range(2):
        for s in range(8):
            if s < 6:
                col = jnp.where(s < count_s[0, t], cols_s[t, 0, s], -1)
                mb[k, t, s, :] = jnp.full((128,), col, jnp.int32)
            else:
                mb[k, t, s, :] = jnp.full((128,), -1, jnp.int32)
    own_a = pltpu.make_async_copy(a_ref, ab.at[k], own_sem.at[0])
    own_b = pltpu.make_async_copy(b_ref, bb.at[k], own_sem.at[1])
    own_a.start()
    own_b.start()

    def wait_for(ref, sem):
        pltpu.make_async_copy(ref, ref, sem).wait()

    pl.semaphore_wait(barrier, 22)

    sib_meta = remote(mb.at[k], mb.at[k], nsend, nrecv, sibling)
    sib_meta.start()

    def meta_row(i, c):
        w = (v % 8 // 2 * 2 + i + 1) % 8
        remote(
            mb.at[k], mb.at[(x - w // 2 + 4) % 4 * 2 + k], msend, mrecv, (y, z * 8 + w)
        ).start()
        return c

    def meta_col(i, c):
        remote(mb.at[k], mb.at[11 - i], msend, mrecv, (y, vir((z + i) % 4, x, k))).start()
        return c

    lax.fori_loop(1, 7, meta_row, 0)
    lax.fori_loop(1, 4, meta_col, 0)

    left, right = (y, vir(z, xm, k)), (y, vir(z, xp, k))
    below, above = (y, vir(zm, x, k)), (y, vir(zp, x, k))
    low, high = pl.ds(0, 512), pl.ds(512, 512)
    one, two, three = 2 + k, 4 + k, 6 + k

    def ahop(n, src, slot, t, dev):
        return remote(src, ab.at[slot, t], asend.at[n], arecv.at[slot, t], dev)

    def bhop(n, src, slot, dev):
        return remote(src, bb.at[slot], bsend.at[n], brecv.at[slot], dev)

    def ahalf(n, src, slot, t, dev):
        return remote(ab.at[src, t], ab.at[slot, t], a2send.at[n], a2recv.at[n], dev)

    def bhalf(n, src, slot, part, dev):
        return remote(src, bb.at[slot, part], b2send.at[n], b2recv.at[n], dev)

    sib_a0 = [ahop(t, a_ref.at[t], k, t, sibling) for t in range(2)]
    sib_b0 = bhop(0, b_ref, k, sibling)
    a_left = [ahop(2 + t, a_ref.at[t], one, t, left) for t in range(2)]
    a_right = [ahop(4 + t, a_ref.at[t], three, t, right) for t in range(2)]
    a_below = [ahop(6 + t, a_ref.at[t], 8, t, below) for t in range(2)]
    a_above = [ahop(8 + t, a_ref.at[t], 10, t, above) for t in range(2)]
    sib_a1 = [ahop(10 + t, ab.at[one, t], one, t, sibling) for t in range(2)]
    sib_a3 = [ahop(12 + t, ab.at[three, t], three, t, sibling) for t in range(2)]
    sib_a2 = [ahop(14 + t, ab.at[two, t], two, t, sibling) for t in range(2)]
    b_left = bhop(1, b_ref, one, left)
    b_below = bhop(2, b_ref, 6, below)
    b_above = bhop(3, b_ref, 8, above)
    sib_b1 = bhop(4, bb.at[one], one, sibling)
    sib_b2 = bhop(5, bb.at[two], two, sibling)
    far_a1 = ahalf(0, one, two, 0, left)
    far_a3 = ahalf(1, three, two, 1, right)
    far_az1 = ahalf(2, 8, 9, 0, below)
    far_az3 = ahalf(3, 10, 9, 1, above)
    far_bz1 = bhalf(0, bb.at[6, low], 7, low, below)
    far_bz3 = bhalf(1, bb.at[8, high], 7, high, above)
    far_b1 = bhalf(2, bb.at[one, low], two, low, left)
    far_b3 = bhalf(3, relay, two, high, right)
    b_relay = remote(b_ref.at[high], relay, rsend, rrecv, right)
    sends = (
        *sib_a0, sib_b0, a_left[1], a_right[1], *a_below, *a_above, *sib_a1, *sib_a3, *sib_a2,
        b_left, b_below, b_above, sib_b1, sib_b2, far_a1, far_a3, far_az1, far_az3,
        far_bz1, far_bz3, far_b1, far_b3, b_relay, sib_meta,
    )

    def got_a(slot, t):
        wait_for(ab.at[slot, t], arecv.at[slot, t])

    def got_b(slot):
        wait_for(bb.at[slot], brecv.at[slot])

    sib_a0[0].start()
    a_left[0].start()
    a_right[0].start()
    sib_b0.start()
    sib_a0[1].start()
    b_below.start()
    b_above.start()
    own_a.wait()
    own_b.wait()

    def dense(slot, t, high_ref, low_ref, at):
        rows = pl.ds(pl.multiple_of(at * 128, 128), 128)
        for col in range(8):
            val = jnp.zeros((128, 128), jnp.float32)
            for s in range(6):
                hit = mb[slot, t, pl.ds(s, 1), :] == col
                val = jnp.where(hit, ab[slot, t, s], val)
            hi = val.astype(jnp.bfloat16)
            lo = (val - hi.astype(jnp.float32)).astype(jnp.bfloat16)
            high_ref[rows, col * 128:(col + 1) * 128] = hi
            low_ref[rows, col * 128:(col + 1) * 128] = lo

    def prep_a_rows(n):
        def body(kk, c):
            dense(n // 2 * 2 + kk, n % 2, aph.at[n], apl.at[n], kk)
            return c

        lax.fori_loop(0, 2, body, 0)

    def prep_a_side(d):
        def body(t, c):
            dense(jnp.where(d == 0, k, 7 + d), t, aqh.at[d], aql.at[d], t)
            return c

        lax.fori_loop(0, 2, body, 0)

    def prep_b_rows(d):
        def body(n, c):
            at = pl.ds(pl.multiple_of(n * 128, 128), 128)
            for kk in range(2):
                for t in range(2):
                    val = bb[d * 2 + kk, at, t * 128:(t + 1) * 128]
                    hi = val.astype(jnp.bfloat16)
                    bph[d * 2 + t, at, kk * 128:(kk + 1) * 128] = hi
                    bpl[d * 2 + t, at, kk * 128:(kk + 1) * 128] = (val - hi.astype(jnp.float32)).astype(jnp.bfloat16)
            return c

        lax.fori_loop(0, 8, body, 0)

    def prep_b_side(d):
        def body(n, c):
            at = pl.ds(pl.multiple_of(n * 128, 128), 128)
            val = bb[jnp.where(d == 0, k, 5 + d), at, :]
            hi = val.astype(jnp.bfloat16)
            bqh[d, at, :] = hi
            bql[d, at, :] = (val - hi.astype(jnp.float32)).astype(jnp.bfloat16)
            return c

        lax.fori_loop(0, 8, body, 0)

    def prepare(s, plan, work):
        n = planned(s, plan)

        @pl.when(n >= 0)
        def _():
            work(n)

    def pair_bits(q, odd):
        one, two = ((q + 1) // 2) % 2, q // 2
        return one + odd * (two - one), two + odd * (one - two)

    def partners(odd):
        near, far = y + 1 - 2 * (y % 2), 3 - y
        return near + odd * (far - near), far + odd * (near - far)

    def first_stage(u):
        return remote(
            p.at[u, 0], r1.at[u], s1send, s1recv.at[u], (partners(u % 2)[0], v)
        )

    def second_stage(u):
        return remote(
            p.at[u, 1, 0], r2.at[u], s2send, s2recv.at[u], (partners(u % 2)[1], v)
        )

    def product(ah, al, wh, wl):
        acc = jnp.dot(ah, wh, preferred_element_type=jnp.float32)
        acc += jnp.dot(ah, wl, preferred_element_type=jnp.float32)
        return acc + jnp.dot(al, wh, preferred_element_type=jnp.float32)

    def compute(u):
        n, db = table(u, DX) * 2 + table(u, DT), table(u, DZ)
        odd = u % 2
        b1, b2 = pair_bits(y, odd)

        def places():
            for q in range(4):
                q1, q2 = pair_bits(q, odd)
                for kk in range(2):
                    yield 1 - (q1 + b1) % 2, 1 - (q2 + b2) % 2, kk, kk * 128 + q * 32

        acc = product(aph[n], apl[n], bqh[db], bql[db])
        for h, w, kk, row in places():
            p[u, h, w, kk] = acc[row:row + 32]

        @pl.when(table(u, BOTH) == 1)
        def _():
            acc = product(aqh[db], aql[db], bph[n], bpl[n]).T
            for h, w, kk, row in places():
                p[u, h, w, kk] += acc[row:row + 32]

    def finish(u):
        da, db, t = table(u, DX), table(u, DZ), table(u, DT)
        zz, xx = (z + db) % 4, (x + da) % 4
        total = p[u, 1, 1] + r2[u]
        p[u, 1, 1] = total
        columns = pl.ds(pl.multiple_of(vir(zz, x, k) * 256, 256), 256)
        for kk in range(2):
            src = p.at[u, 1, 1, kk]
            dst = direct.at[t, :, columns]
            here = jnp.logical_and(da == 0, k == kk)

            @pl.when(here)
            def _():
                pltpu.make_async_copy(src, dst, drecv).start()

            @pl.when(jnp.logical_not(here))
            def _():
                remote(src, dst, dsend, drecv, (y, vir(z, xx, kk))).start()

        place = y * 16 + z * 4 + xx

        @pl.when(table(u, TURN) == 1)
        def _():
            mate = table(u, MATE)
            rows = [p[mate, 1, 1, 0], total[0], p[mate, 1, 1, 1], total[1]]
            slot = table(u, [sum(TURN[:i]) for i in range(UNITS)])
            ft[slot] = jnp.concatenate(rows, axis=0).T.reshape(2, 4, 32, 128)
            for q in range(4):
                src = ft.at[slot, :, q]
                dst = stg.at[place]
                here = jnp.logical_and(db == 0, y == q)

                @pl.when(here)
                def _():
                    pltpu.make_async_copy(src, dst, trecv).start()

                @pl.when(jnp.logical_not(here))
                def _():
                    remote(src, dst, tsend, trecv, (q, vir(zz, x, k))).start()

    def step(s, c):
        @pl.when(s < UNITS)
        def _():
            @pl.when(s == 0)
            def _():
                sib_meta.wait_recv()
                got_a(other, 0)
                got_a(other, 1)
                got_b(other)

            @pl.when(s == 2)
            def _():
                a_left[0].wait_send()
                a_left[1].start()
                a_right[0].wait_send()
                a_right[1].start()
                wait_for(mb.at[pl.ds(0, 9)], mrecv)
                got_a(one, 0)
                sib_a1[0].start()
                got_a(three, 0)
                sib_a3[0].start()
                got_a(2 + other, 0)

            @pl.when(s == 3)
            def _():
                got_a(6 + other, 0)

            @pl.when(s == 4)
            def _():
                got_a(one, 1)
                far_a1.start()
                sib_a1[1].start()
                got_a(three, 1)
                far_a3.start()
                sib_a3[1].start()
                got_a(2 + other, 1)

            @pl.when(s == 5)
            def _():
                b_left.start()
                b_relay.start()
                got_a(6 + other, 1)
                got_b(6)
                far_bz1.start()
                got_b(8)
                far_bz3.start()

            @pl.when(s == 6)
            def _():
                far_a1.wait_recv()
                sib_a2[0].start()
                far_a3.wait_recv()
                sib_a2[1].start()
                got_a(4 + other, 0)

            @pl.when(s == 7)
            def _():
                for copy in (*a_below, *a_above):
                    copy.start()
                got_a(4 + other, 1)

            @pl.when(s == 8)
            def _():
                far_bz1.wait_recv()
                far_bz3.wait_recv()

            @pl.when(s == 11)
            def _():
                b_relay.wait_recv()
                far_b3.start()

            @pl.when(s == 12)
            def _():
                got_b(one)
                far_b1.start()
                sib_b1.start()
                for t in range(2):
                    got_a(8, t)
                    got_a(10, t)
                far_az1.start()
                far_az3.start()

            @pl.when(s == 14)
            def _():
                got_b(2 + other)

            @pl.when(s == 18)
            def _():
                far_az1.wait_recv()
                far_az3.wait_recv()

            @pl.when(s == 20)
            def _():
                far_b1.wait_recv()
                far_b3.wait_recv()
                sib_b2.start()
                got_b(4 + other)

            prepare(s, A_ROWS, prep_a_rows)
            prepare(s, A_SIDE, prep_a_side)
            prepare(s, B_ROWS, prep_b_rows)
            prepare(s, B_SIDE, prep_b_side)
            compute(s)
            first_stage(s).start()

        @pl.when(jnp.logical_and(s >= LAG1, s < LAG1 + UNITS))
        def _():
            u = s - LAG1
            first_stage(u).wait_recv()
            p[u, 1] += r1[u]
            second_stage(u).start()

        @pl.when(s >= LAG2)
        def _():
            u = s - LAG2
            second_stage(u).wait_recv()
            finish(u)

        return c

    lax.fori_loop(0, UNITS + LAG2, step, 0)

    for copy in sends:
        copy.wait_send()
    wait_for(mb.at[pl.ds(0, 9)], msend)
    wait_for(r1, s1send)
    wait_for(r2, s2send)
    home = sum(1 for a in DX if a == 0)
    turned_home = sum(1 for b, t in zip(DZ, TURN) if b == 0 and t)
    wait_for(direct.at[:, :, pl.ds(0, (UNITS - home // 2) * 256)], dsend)
    wait_for(stg.at[pl.ds(0, 4 * sum(TURN) - turned_home)], tsend)

    wait_for(direct.at[:, :, pl.ds(0, UNITS * 256)], drecv)
    wait_for(stg.at[pl.ds(0, 4 * sum(TURN))], trecv)
    group = lax.broadcasted_iota(jnp.int32, (32, 128), 1) // 32
    summed, _, only_turned = covers()

    def assemble(pairs, add):
        pairs = sorted(pairs)

        def body(n, c):
            xx = (x + table(n, [a for a, _ in pairs])) % 4
            zz = (z + table(n, [b for _, b in pairs])) % 4
            g = zz * 4 + xx
            for t in range(2):
                parts = [stg[16 * n + g, t] for n in range(4)]
                for n in range(4):
                    merged = parts[n]
                    for src in range(4):
                        if src != n:
                            merged = jnp.where(group == src, pltpu.roll(parts[src], (32 * (src - n)) % 128, 1), merged)
                    columns = pl.ds(pl.multiple_of(g * 512 + n * 128, 128), 128)
                    direct[t, :, columns] = direct[t, :, columns] + merged if add else merged
            return c

        if pairs:
            lax.fori_loop(0, len(pairs), body, 0)

    assemble(summed, True)
    assemble(only_turned, False)
    out = pltpu.make_async_copy(direct, out_ref, own_sem.at[0])
    out.start()
    out.wait()


def on_device(amplitudes, tile_cols, tile_count, integrals, residual_in):
    vmem = pl.BlockSpec(memory_space=pltpu.VMEM)
    smem = pl.BlockSpec(memory_space=pltpu.SMEM)
    f32, bf16 = jnp.float32, jnp.bfloat16
    dma = pltpu.SemaphoreType.DMA
    added = pl.pallas_call(
        kernel,
        out_shape=jax.ShapeDtypeStruct(residual_in.shape, f32),
        in_specs=[smem, smem, vmem, vmem],
        out_specs=pl.BlockSpec(memory_space=pl.ANY),
        scratch_shapes=[
            pltpu.VMEM((11, 2, 6, 128, 128), f32),
            pltpu.VMEM((11, 2, 8, 128), jnp.int32),
            pltpu.VMEM((9, 1024, 256), f32),
            pltpu.VMEM((512, 256), f32),
            pltpu.VMEM((8, 256, 1024), bf16),
            pltpu.VMEM((8, 256, 1024), bf16),
            pltpu.VMEM((4, 256, 1024), bf16),
            pltpu.VMEM((4, 256, 1024), bf16),
            pltpu.VMEM((6, 1024, 256), bf16),
            pltpu.VMEM((6, 1024, 256), bf16),
            pltpu.VMEM((4, 1024, 256), bf16),
            pltpu.VMEM((4, 1024, 256), bf16),
            pltpu.VMEM((UNITS, 2, 2, 2, 32, 256), f32),
            pltpu.VMEM((UNITS, 2, 2, 32, 256), f32),
            pltpu.VMEM((UNITS, 2, 32, 256), f32),
            pltpu.VMEM((sum(TURN), 2, 4, 32, 128), f32),
            pltpu.VMEM((2, 32, 8192), f32),
            pltpu.VMEM((64, 2, 32, 128), f32),
            dma((2,)), dma((16,)), dma((11, 2)), dma((4,)), dma((4,)), dma, dma, dma, dma,
            dma((6,)), dma((9,)), dma((4,)), dma((4,)), dma, dma,
            dma, dma((UNITS,)), dma, dma((UNITS,)), dma, dma, dma, dma,
        ],
        compiler_params=pltpu.CompilerParams(
            collective_id=0, has_side_effects=True, vmem_limit_bytes=60 * 1024 * 1024
        ),
        cost_estimate=pl.CostEstimate(flops=10 * 10**9, bytes_accessed=6 * 10**6, transcendentals=0),
    )(tile_cols, tile_count.T, amplitudes[:, 0], integrals)
    return residual_in + added


def solution(mesh):
    in_specs = (
        P("vir", "occ", None, None, None),
        P("vir", "occ", None),
        P("vir", "occ"),
        P("occ", "vir"),
        P("vir", "occ", None),
    )
    out_specs = P("vir", "occ", None)
    return jax.shard_map(
        on_device, mesh=mesh, in_specs=in_specs, out_specs=out_specs, check_vma=False
    )
```

time: 119 us -> 112 us (0.941)
  Pallas kernels: 114 us -> 109 us
  local copies, waits for them, and re-layouts: 1.3 us -> 0.01 us
    pallas_call x1, Pallas kernels: 114 us -> 109 us  [on_device(): pl.pallas_call(kernel, out_shape=jax.ShapeDtypeStruct(residual_in.shape,...]
    unnamed x3 -> x2, local copies, waits for them, and re-layouts: 1.3 us -> 0.01 us
where the time goes in v3:
time: 112 us
  Pallas kernels  109 us (97%)
  other arithmetic  3.12 us (3%)
    pallas_call x1, Pallas kernels, on_device(): pl.pallas_call(kernel, out_shape=jax.ShapeDtypeStruct(residual_in.shape,...  109 us
    add x1, other arithmetic, on_device(): return residual_in + added  3.12 us

profile of v3, /device:TPU:1, one launch (start us, length us, event | category | flops | bytes accessed | tf_op | source)
XLA Modules:
  0.0 112.2 jit_solution(8615370878958318809)
XLA Ops:
  0.0 0.0 copy-start
  0.0 109.0 %shard_map.55 = f32[2,32,8192]{2,1,0:T(8,128)} custom-call(s32[2,1,6]{2,1,0:T(1,128)} %cols_s.1, s32[1,2]{1,0:T(1,128)} %bitcast.3, f32[2,6,128,128]{3,2,1,0:T(8,128)} %bitcast.2, f32[1024,256]{1,0:T(8,128)} %b_ref.1), custom_call_target="tpu_custom_call" | custom-call | flops 10000000000 | bytes 6000000 | tf_op jit(solution)/shard_map/pallas_call | solution.py:492
  109.0 0.0 copy-done
  109.0 3.1 %add.3 = f32[2,32,8192]{2,1,0:T(8,128)} add(f32[2,32,8192]{2,1,0:T(8,128)S(1)} %copy-done, f32[2,32,8192]{2,1,0:T(8,128)} %shard_map.55) | non-fusion elementwise | flops 524288 | bytes 6291456 | tf_op jit(solution)/shard_map/add | solution.py:525
Async XLA Ops:
  0.0 109.0 %copy-start = (f32[2,32,8192]{2,1,0:T(8,128)S(1)}, f32[2,32,8192]{2,1,0:T(8,128)}, u32[]{:S(2)}) copy-start(f32[2,32,8192]{2,1,0:T(8,128)} %param.9) | copy-start | bytes 6291460

commit v4 on v3

--- a/solution.py
+++ b/solution.py
@@ -8,19 +8,19 @@
 MESH = pl.DeviceIdType.MESH
 LAG1 = 2
 LAG2 = 4
-DX = (0, 0, 1, 3, 1, 3, 2, 2, 0, 0, 2, 2, 0, 0, 1, 1, 1, 1, 1, 1, 2, 2)
-DZ = (0, 0, 0, 0, 0, 0, 0, 0, 2, 2, 2, 2, 1, 1, 1, 1, 3, 3, 2, 2, 1, 1)
-DT = (0, 1, 0, 0, 1, 1, 0, 1, 0, 1, 0, 1, 0, 1, 0, 1, 0, 1, 0, 1, 0, 1)
+DX = (0, 0, 1, 3, 1, 3, 2, 2, 2, 2, 2, 2, 0, 0, 2, 2, 0, 0, 1, 1, 1, 1, 1, 1)
+DZ = (0, 0, 0, 0, 0, 0, 0, 0, 1, 1, 3, 3, 2, 2, 2, 2, 1, 1, 1, 1, 3, 3, 2, 2)
+DT = (0, 1, 0, 0, 1, 1, 0, 1, 0, 1, 0, 1, 0, 1, 0, 1, 0, 1, 0, 1, 0, 1, 0, 1)
 MATE = tuple(
     next(j for j in range(len(DX)) if j != i and DX[j] == DX[i] and DZ[j] == DZ[i])
     for i in range(len(DX))
 )
-BOTH = (1, 1) + (0,) * 10 + (1,) * 10
+BOTH = (1, 1) + (0,) * 14 + (1,) * 8
 TURN = (0, 0) + DT[2:]
 A_ROWS = {0: 0, 1: 1, 2: 2, 3: 6, 4: 3, 5: 7, 6: 4, 7: 5}
-A_SIDE = {0: 0, 12: 1, 16: 3, 18: 2}
-B_ROWS = {0: 0, 14: 1, 20: 2}
-B_SIDE = {0: 0, 8: 2, 12: 1, 16: 3}
+A_SIDE = {0: 0, 16: 1, 20: 3, 22: 2}
+B_ROWS = {0: 0, 18: 1}
+B_SIDE = {0: 0, 8: 1, 10: 3, 12: 2}
 UNITS = len(DX)
 
 
@@ -44,8 +44,8 @@
 
 def kernel(
     cols_s, count_s, a_ref, b_ref, out_ref,
-    ab, mb, bb, relay, aph, apl, aqh, aql, bph, bpl, bqh, bql, p, r1, r2, ft, direct, stg,
-    own_sem, asend, arecv, a2send, a2recv, msend, mrecv, nsend, nrecv, bsend, brecv, b2send, b2recv, rsend, rrecv,
+    ab, mb, bb, aph, apl, aqh, aql, bph, bpl, bqh, bql, p, r1, r2, ft, direct, stg,
+    own_sem, asend, arecv, a2send, a2recv, msend, mrecv, nsend, nrecv, bsend, brecv, b2send, b2recv,
     s1send, s1recv, s2send, s2recv, dsend, drecv, tsend, trecv,
 ):
     y = lax.axis_index("occ")
@@ -143,23 +143,19 @@
     sib_a3 = [ahop(12 + t, ab.at[three, t], three, t, sibling) for t in range(2)]
     sib_a2 = [ahop(14 + t, ab.at[two, t], two, t, sibling) for t in range(2)]
     b_left = bhop(1, b_ref, one, left)
-    b_below = bhop(2, b_ref, 6, below)
-    b_above = bhop(3, b_ref, 8, above)
+    b_below = bhop(2, b_ref, 4, below)
+    b_above = bhop(3, b_ref, 6, above)
     sib_b1 = bhop(4, bb.at[one], one, sibling)
-    sib_b2 = bhop(5, bb.at[two], two, sibling)
     far_a1 = ahalf(0, one, two, 0, left)
     far_a3 = ahalf(1, three, two, 1, right)
     far_az1 = ahalf(2, 8, 9, 0, below)
     far_az3 = ahalf(3, 10, 9, 1, above)
-    far_bz1 = bhalf(0, bb.at[6, low], 7, low, below)
-    far_bz3 = bhalf(1, bb.at[8, high], 7, high, above)
-    far_b1 = bhalf(2, bb.at[one, low], two, low, left)
-    far_b3 = bhalf(3, relay, two, high, right)
-    b_relay = remote(b_ref.at[high], relay, rsend, rrecv, right)
+    far_bz1 = bhalf(0, bb.at[4, low], 5, low, below)
+    far_bz3 = bhalf(1, bb.at[6, high], 5, high, above)
     sends = (
         *sib_a0, sib_b0, a_left[1], a_right[1], *a_below, *a_above, *sib_a1, *sib_a3, *sib_a2,
-        b_left, b_below, b_above, sib_b1, sib_b2, far_a1, far_a3, far_az1, far_az3,
-        far_bz1, far_bz3, far_b1, far_b3, b_relay, sib_meta,
+        b_left, b_below, b_above, sib_b1, far_a1, far_a3, far_az1, far_az3,
+        far_bz1, far_bz3, sib_meta,
     )
 
     def got_a(slot, t):
@@ -220,7 +216,7 @@
     def prep_b_side(d):
         def body(n, c):
             at = pl.ds(pl.multiple_of(n * 128, 128), 128)
-            val = bb[jnp.where(d == 0, k, 5 + d), at, :]
+            val = bb[jnp.where(d == 0, k, 3 + d), at, :]
             hi = val.astype(jnp.bfloat16)
             bqh[d, at, :] = hi
             bql[d, at, :] = (val - hi.astype(jnp.float32)).astype(jnp.bfloat16)
@@ -359,11 +355,10 @@
             @pl.when(s == 5)
             def _():
                 b_left.start()
-                b_relay.start()
                 got_a(6 + other, 1)
+                got_b(4)
+                far_bz1.start()
                 got_b(6)
-                far_bz1.start()
-                got_b(8)
                 far_bz3.start()
 
             @pl.when(s == 6)
@@ -376,24 +371,21 @@
 
             @pl.when(s == 7)
             def _():
+                got_a(4 + other, 1)
+
+            @pl.when(s == 10)
+            def _():
+                far_bz1.wait_recv()
+                far_bz3.wait_recv()
+
+            @pl.when(s == 8)
+            def _():
                 for copy in (*a_below, *a_above):
                     copy.start()
-                got_a(4 + other, 1)
-
-            @pl.when(s == 8)
-            def _():
-                far_bz1.wait_recv()
-                far_bz3.wait_recv()
-
-            @pl.when(s == 11)
-            def _():
-                b_relay.wait_recv()
-                far_b3.start()
-
-            @pl.when(s == 12)
+
+            @pl.when(s == 15)
             def _():
                 got_b(one)
-                far_b1.start()
                 sib_b1.start()
                 for t in range(2):
                     got_a(8, t)
@@ -401,21 +393,14 @@
                 far_az1.start()
                 far_az3.start()
 
-            @pl.when(s == 14)
+            @pl.when(s == 18)
             def _():
                 got_b(2 + other)
 
-            @pl.when(s == 18)
+            @pl.when(s == 22)
             def _():
                 far_az1.wait_recv()
                 far_az3.wait_recv()
-
-            @pl.when(s == 20)
-            def _():
-                far_b1.wait_recv()
-                far_b3.wait_recv()
-                sib_b2.start()
-                got_b(4 + other)
 
             prepare(s, A_ROWS, prep_a_rows)
             prepare(s, A_SIDE, prep_a_side)
@@ -497,14 +482,13 @@
         scratch_shapes=[
             pltpu.VMEM((11, 2, 6, 128, 128), f32),
             pltpu.VMEM((11, 2, 8, 128), jnp.int32),
-            pltpu.VMEM((9, 1024, 256), f32),
-            pltpu.VMEM((512, 256), f32),
+            pltpu.VMEM((7, 1024, 256), f32),
             pltpu.VMEM((8, 256, 1024), bf16),
             pltpu.VMEM((8, 256, 1024), bf16),
             pltpu.VMEM((4, 256, 1024), bf16),
             pltpu.VMEM((4, 256, 1024), bf16),
-            pltpu.VMEM((6, 1024, 256), bf16),
-            pltpu.VMEM((6, 1024, 256), bf16),
+            pltpu.VMEM((4, 1024, 256), bf16),
+            pltpu.VMEM((4, 1024, 256), bf16),
             pltpu.VMEM((4, 1024, 256), bf16),
             pltpu.VMEM((4, 1024, 256), bf16),
             pltpu.VMEM((UNITS, 2, 2, 2, 32, 256), f32),
@@ -514,7 +498,7 @@
             pltpu.VMEM((2, 32, 8192), f32),
             pltpu.VMEM((64, 2, 32, 128), f32),
             dma((2,)), dma((16,)), dma((11, 2)), dma((4,)), dma((4,)), dma, dma, dma, dma,
-            dma((6,)), dma((9,)), dma((4,)), dma((4,)), dma, dma,
+            dma((5,)), dma((7,)), dma((2,)), dma((2,)),
             dma, dma((UNITS,)), dma, dma((UNITS,)), dma, dma, dma, dma,
         ],
         compiler_params=pltpu.CompilerParams(

time: 112 us -> 111 us (level)
  Pallas kernels: 109 us -> 107 us
    pallas_call x1, Pallas kernels: 109 us -> 107 us  [on_device(): pl.pallas_call(kernel, out_shape=jax.ShapeDtypeStruct(residual_in.shape,...]
where the time goes in v4:
time: 111 us; the launch traced here: 110 us
  Pallas kernels  107 us (96%)
  other arithmetic  3.12 us (3%)
    pallas_call x1, Pallas kernels, on_device(): pl.pallas_call(kernel, out_shape=jax.ShapeDtypeStruct(residual_in.shape,...  107 us
    add x1, other arithmetic, on_device(): return residual_in + added  3.12 us

profile of v4, /device:TPU:1, one launch (start us, length us, event | category | flops | bytes accessed | tf_op | source)
XLA Modules:
  0.0 110.4 jit_solution(6994109631097513667)
XLA Ops:
  0.0 0.0 copy-start
  0.0 107.3 %shard_map.55 = f32[2,32,8192]{2,1,0:T(8,128)} custom-call(s32[2,1,6]{2,1,0:T(1,128)} %cols_s.1, s32[1,2]{1,0:T(1,128)} %bitcast.3, f32[2,6,128,128]{3,2,1,0:T(8,128)} %bitcast.2, f32[1024,256]{1,0:T(8,128)} %b_ref.1), custom_call_target="tpu_custom_call" | custom-call | flops 10000000000 | bytes 6000000 | tf_op jit(solution)/shard_map/pallas_call | solution.py:477
  107.3 0.0 copy-done
  107.3 3.1 %add.3 = f32[2,32,8192]{2,1,0:T(8,128)} add(f32[2,32,8192]{2,1,0:T(8,128)S(1)} %copy-done, f32[2,32,8192]{2,1,0:T(8,128)} %shard_map.55) | non-fusion elementwise | flops 524288 | bytes 6291456 | tf_op jit(solution)/shard_map/add | solution.py:509
Async XLA Ops:
  0.0 107.3 %copy-start = (f32[2,32,8192]{2,1,0:T(8,128)S(1)}, f32[2,32,8192]{2,1,0:T(8,128)}, u32[]{:S(2)}) copy-start(f32[2,32,8192]{2,1,0:T(8,128)} %param.9) | copy-start | bytes 6291460
